TPU v7x, 32 devices: a whole 2x2x4 slice. The times are simulated.
32 devices in a mesh: groups: 2 (over y), pair: 8 (over z, x), aux: 2 (over core).
Axes of the slice: x: 2, y: 2, z: 4, core: 2. Of those that a mesh axis runs over, the one named last changes fastest.
Arguments:
- factors: float32 [8192, 2048], P(('groups', 'pair', 'aux')), parts along dimension 0, may hold values from -0.6 to 0.6
- occupied_energy: float32 [256], P('groups'), parts along dimension 0, may hold values from -3 to -0.4
- virtual_energy: float32 [4096], P('groups'), parts along dimension 0, may hold values from 0.2 to 4
- batch_orbitals: int32 [2], P('groups'), parts along dimension 0, may hold values from 0 to 127, as said below
- panel_order: int32 [32], P('groups'), parts along dimension 0, may hold values from 0 to 31, as said below
Outputs:
- density: float32 [8192, 2048], P(('groups', 'pair', 'aux')), parts along dimension 0
There are 2 independent parts, one for each index of `groups`. A program takes and returns all parts, laid end to end along the dimension named above; each array names one. Nothing has to cross between parts.
Inputs may be any that keep to these rules, and one draw needn't show every extreme that they name: `batch_orbitals`: 1 distinct occupied orbitals. `panel_order`: 16 distinct panel numbers.
All inputs are finite; a program needn't handle non-finite values.
Results may differ from a plain program's by a relative error of at most 0.0001.
Values sent between devices are 32-bit elements; how exact they have to be, the bound alone decides.
A program may use at most 64 MiB of HBM per device.

v0:
```python
import jax
import jax.numpy as jnp
from jax import lax
from jax.sharding import PartitionSpec as P

PANEL = 64
os_scale = 1.3


def spread(block, axis, source):
    block = jnp.where(lax.axis_index(axis) == source, block, jnp.zeros_like(block))
    return lax.psum(block, axis)


def column_energies(columns, batch_energy, virtual_energy):
    nvir = virtual_energy.shape[0]
    nbatch = batch_energy.shape[0]
    orbital = columns // nvir
    virtual = columns % nvir
    occ_part = jnp.sum(
        jnp.where(
            orbital[:, None] == jnp.arange(nbatch, dtype=jnp.int32)[None, :],
            batch_energy[None, :],
            0.0,
        ),
        axis=1,
    )
    vir_part = jnp.sum(
        jnp.where(
            virtual[:, None] == jnp.arange(nvir, dtype=jnp.int32)[None, :],
            virtual_energy[None, :],
            0.0,
        ),
        axis=1,
    )
    return vir_part - occ_part


def batch_energies(occupied_energy, batch_orbitals):
    noccupied = occupied_energy.shape[0]
    return jnp.sum(
        jnp.where(
            batch_orbitals[:, None] == jnp.arange(noccupied, dtype=jnp.int32)[None, :],
            occupied_energy[None, :],
            0.0,
        ),
        axis=1,
    )


def by_columns(factors, occupied_energy, virtual_energy, batch_orbitals, panel_order):
    pair_count = lax.axis_size("pair")
    total_columns = factors.shape[1]
    col_local = total_columns // pair_count
    per_owner = col_local // PANEL
    working = lax.all_to_all(factors, "pair", split_axis=1, concat_axis=0, tiled=True)
    batch_energy = batch_energies(occupied_energy, batch_orbitals)
    own_columns = lax.axis_index("pair") * col_local + jnp.arange(col_local, dtype=jnp.int32)
    own_energy = column_energies(own_columns, batch_energy, virtual_energy)

    def one_panel(position, density):
        number = panel_order[position]
        owner_index = number // per_owner
        panel_slab = lax.dynamic_slice_in_dim(working, number % per_owner * PANEL, PANEL, 1)
        panel_block = spread(panel_slab, "pair", owner_index)
        panel_energy = column_energies(
            number * PANEL + jnp.arange(PANEL, dtype=jnp.int32), batch_energy, virtual_energy
        )
        partial_ints = lax.dot_general(
            panel_block,
            working,
            (((0,), (0,)), ((), ())),
            precision=lax.Precision.HIGHEST,
            preferred_element_type=jnp.float32,
        )
        integrals = lax.psum(partial_ints, "aux")
        amplitudes = os_scale * integrals / (own_energy[None, :] + panel_energy[:, None])
        return density + jnp.dot(
            panel_block,
            amplitudes,
            precision=lax.Precision.HIGHEST,
            preferred_element_type=jnp.float32,
        )

    density = lax.fori_loop(
        0, panel_order.shape[0], one_panel, jnp.zeros(working.shape, jnp.float32)
    )
    return lax.all_to_all(density, "pair", split_axis=0, concat_axis=1, tiled=True)


def by_rows(factors, occupied_energy, virtual_energy, batch_orbitals, panel_order):
    total = factors.shape[1]
    batch_energy = batch_energies(occupied_energy, batch_orbitals)
    nvir = virtual_energy.shape[0]
    energy = (virtual_energy[None, :] - batch_energy[:, None]).reshape(-1)
    panels = jnp.concatenate(
        [
            lax.dynamic_slice_in_dim(factors, panel_order[k] * PANEL, PANEL, 1)
            for k in range(panel_order.shape[0])
        ],
        axis=1,
    )
    chosen = jnp.concatenate(
        [
            lax.dynamic_slice_in_dim(energy, panel_order[k] * PANEL, PANEL, 0)
            for k in range(panel_order.shape[0])
        ]
    )
    partial = lax.dot_general(
        panels,
        factors,
        (((0,), (0,)), ((), ())),
        precision=lax.Precision.HIGH,
        preferred_element_type=jnp.float32,
    )
    mine = lax.psum_scatter(partial, ("pair", "aux"), scatter_dimension=0, tiled=True)
    rank = lax.axis_index("pair") * lax.axis_size("aux") + lax.axis_index("aux")
    my_energy = lax.dynamic_slice_in_dim(chosen, rank * mine.shape[0], mine.shape[0], 0)
    mine = os_scale * mine / (energy[None, :] + my_energy[:, None])
    amplitudes = lax.all_gather(mine, ("pair", "aux"), axis=0, tiled=True)
    return jnp.dot(
        panels, amplitudes, precision=lax.Precision.HIGH, preferred_element_type=jnp.float32
    )


def on_device(factors, occupied_energy, virtual_energy, batch_orbitals, panel_order):
    window = panel_order.shape[0] * PANEL
    fits = 4 * window * factors.shape[1] <= 8 * 1024 * 1024
    plan = by_rows if fits else by_columns
    return plan(factors, occupied_energy, virtual_energy, batch_orbitals, panel_order)


def solution(mesh):
    in_specs = (
        P(("groups", "pair", "aux"), None),
        P("groups"),
        P("groups"),
        P("groups"),
        P("groups"),
    )
    out_specs = P(("groups", "pair", "aux"), None)
    return jax.shard_map(
        on_device, mesh=mesh, in_specs=in_specs, out_specs=out_specs, check_vma=False
    )
```

profile of v0, /device:TPU:0, one launch (start us, length us, event | category | flops | bytes accessed | tf_op | source)
XLA Modules:
  0.0 228.8 jit_solution(1374346407316018232)
XLA Ops:
  6.5 0.0 reduce-scatter.2.cloned.1.call-start
  6.5 2.0 fusion.2
  18.7 3.4 %constant_dynamic-slice_fusion = (f32[256,64]{1,0:T(8,128)S(1)}, f32[256,64]{1,0:T(8,128)S(1)}, f32[256,64]{1,0:T(8,128)S(1)}, f32[256,64]{1,0:T(8,128)}, f32[25...) fusion(f32[256,2048]{1,0:T(8,128)} %param.5, ...), kind=kLoop, calls=%fused_computation.2 | loop fusion | bytes 2097216 | tf_op jit(solution)/shard_map/dynamic_slice | solution.py:98
  22.1 0.0 copy-start
  22.1 1.9 concatenate.6
  24.0 0.3 copy-done
  24.3 5.8 %fusion.3 = f32[1024,2048]{1,0:T(8,128)} fusion(f32[256,1024]{1,0:T(8,128)S(1)} %concatenate.6, f32[256,2048]{1,0:T(8,128)S(1)} %copy-done), kind=kOutput, calls=%fused_computation.22 | convolution fusion | flops 3221225472 | bytes 11534336 | tf_op jit(solution)/shard_map/dot_general | solution.py:109
  30.1 0.0 copy-start.2
  30.1 0.0 copy-start.1
  30.1 0.0 reduce-scatter.2.cloned.1.call-update
  30.1 0.0 all-gather.2.cloned.1.call-start
  30.8 0.0 copy-done.2
  30.8 0.6 fusion
  31.5 0.0 copy-done.1
  31.5 0.6 broadcast_subtract_fusion
  32.1 0.2 fusion.1
  32.3 0.1 concatenate.7
  32.3 0.1 dynamic_slice.131
  32.4 105.1 %reduce-scatter.2.cloned.1.call-done = f32[64,2048]{1,0:T(8,128)} async-done(((f32[1024,2048]{1,0:T(8,128)}), f32[64,2048]{1,0:T(8,128)}) %reduce-scatter.2.cloned.1.call-update) | async-done | bytes 524304 | tf_op jit(solution)/shard_map/reduce_scatter | solution.py:116
  137.6 2.0 add_divide_fusion
  139.6 0.0 all-gather.2.cloned.1.call-update
  139.6 74.8 %all-gather.2.cloned.1.call-done = f32[1024,2048]{1,0:T(8,128)} async-done(((f32[64,2048]{1,0:T(8,128)}), f32[1024,2048]{1,0:T(8,128)}) %all-gather.2.cloned.1.call-update) | async-done | bytes 8388624 | tf_op jit(solution)/shard_map/all_gather | solution.py:120
  214.4 7.6 %fusion.4 = f32[256,2048]{1,0:T(8,128)} fusion(f32[256,1024]{1,0:T(8,128)S(1)} %concatenate.6, f32[1024,2048]{1,0:T(8,128)} %all-gather.2.cloned.1.call-done), kind=kOutput, calls=%fused_computation.23 | convolution fusion | flops 3221225472 | bytes 11534336 | tf_op jit(solution)/shard_map/dot_general | solution.py:121
Async XLA Ops:
  6.5 131.0 %reduce-scatter.2.cloned.1.call-start = ((), (), s32[]{:S(2)}) async-start(), calls=%async_computation.1 | async-start | bytes 8912896 | tf_op jit(solution)/shard_map/reduce_scatter | solution.py:116
  22.1 2.2 copy-start
  30.1 0.7 copy-start.2
  30.1 1.4 copy-start.1
  30.1 184.3 %all-gather.2.cloned.1.call-start = ((), (), s32[]{:S(2)}) async-start(), calls=%async_computation.2 | async-start | bytes 8912896 | tf_op jit(solution)/shard_map/all_gather | solution.py:120
Sparse Core Ops, SparseCore 0:
  30.2 107.2 reduce-scatter.1
  139.7 74.6 all-gather.1
where the time goes:
time: 229 us
  waiting for transfers between devices  180 us (79%)
  between operations  24.3 us (11%)
  matrix products  13.4 us (6%)
  local copies, waits for them, and re-layouts  7.91 us (3%)
  other arithmetic  3.25 us (1%)
    reduce_scatter x1, waiting for transfers between devices, by_rows(): lax.psum_scatter(partial, ('pair', 'aux'), scatter_dimension=0, tiled=True)  105 us
    all_gather x1, waiting for transfers between devices, by_rows(): amplitudes = lax.all_gather(mine, ('pair', 'aux'), axis=0, tiled=True)  74.8 us
    dot_general x1, matrix products, by_rows(): jnp.dot(panels, amplitudes, precision=lax.Precision.HIGH, preferred_eleme...  7.56 us
    dot_general x1, matrix products, by_rows(): lax.dot_general(panels, factors, (((0,), (0,)), ((), ())), precision=lax....  5.8 us
  transfers between devices with their start and end apart: 2, of which 2 were waited for; matrix products, arithmetic and copies ran while one was open for 1% of the time, Pallas kernels for 0%

commit v1 on v0

--- a/solution.py
+++ b/solution.py
@@ -5,6 +5,23 @@
 
 PANEL = 64
 os_scale = 1.3
+
+
+def joined_along(blocks, dim):
+    shape = list(blocks.shape[1:])
+    shape[dim] *= blocks.shape[0]
+    return jnp.moveaxis(blocks, 0, dim).reshape(shape)
+
+
+def grow_blocks(x, axis):
+    size, index = (lax.axis_size(axis), lax.axis_index(axis))
+    blocks, apart = (x[None], 1)
+    while apart < size:
+        other = lax.ppermute(blocks, axis, [(i, i ^ apart) for i in range(size)])
+        low = index & apart == 0
+        blocks = jnp.concatenate([jnp.where(low, blocks, other), jnp.where(low, other, blocks)])
+        apart *= 2
+    return blocks
 
 
 def spread(block, axis, source):
@@ -117,7 +134,7 @@
     rank = lax.axis_index("pair") * lax.axis_size("aux") + lax.axis_index("aux")
     my_energy = lax.dynamic_slice_in_dim(chosen, rank * mine.shape[0], mine.shape[0], 0)
     mine = os_scale * mine / (energy[None, :] + my_energy[:, None])
-    amplitudes = lax.all_gather(mine, ("pair", "aux"), axis=0, tiled=True)
+    amplitudes = joined_along(grow_blocks(mine, ("pair", "aux")), 0)
     return jnp.dot(
         panels, amplitudes, precision=lax.Precision.HIGH, preferred_element_type=jnp.float32
     )

time: 229 us -> 428 us (1.87)
  waiting for transfers between devices: 180 us -> 356 us
  other arithmetic: 3.25 us -> 21.8 us
  starting transfers between devices: 0.04 us -> 5.39 us
    ppermute x0 -> x4, waiting for transfers between devices: none -> 251 us  [grow_blocks(): other = lax.ppermute(blocks, axis, [(i, i ^ apart) for i in range(size)])]
    all_gather x1 -> x0, waiting for transfers between devices: 74.8 us -> none  [by_rows(): amplitudes = lax.all_gather(mine, ('pair', 'aux'), axis=0, tiled=True)]
    select_n x0 -> x4, other arithmetic: none -> 11.6 us  [grow_blocks(): jnp.where(low, blocks, other)]
    concatenate x0 -> x4, other arithmetic: none -> 7.83 us  [grow_blocks(): jnp.concatenate([jnp.where(low, blocks, other), jnp.where(low, other, blo...]
    ppermute x0 -> x4, starting transfers between devices: none -> 5.39 us  [grow_blocks(): other = lax.ppermute(blocks, axis, [(i, i ^ apart) for i in range(size)])]
  transfers between devices with their start and end apart: 2 -> 5, of which waited for: 2 -> 5; matrix products, arithmetic and copies ran while one was open for 1% -> 0% of each run, Pallas kernels for 0% -> 0%
where the time goes in v1:
time: 428 us
  waiting for transfers between devices  356 us (83%)
  between operations  24.4 us (6%)
  other arithmetic  21.8 us (5%)
  matrix products  11 us (3%)
  local copies, waits for them, and re-layouts  8.77 us (2%)
  starting transfers between devices  5.39 us (1%)
    ppermute x4, waiting for transfers between devices, grow_blocks(): other = lax.ppermute(blocks, axis, [(i, i ^ apart) for i in range(size)])  251 us
    reduce_scatter x1, waiting for transfers between devices, by_rows(): lax.psum_scatter(partial, ('pair', 'aux'), scatter_dimension=0, tiled=True)  105 us
    select_n x4, other arithmetic, grow_blocks(): jnp.where(low, blocks, other)  11.6 us
  transfers between devices with their start and end apart: 5, of which 5 were waited for; matrix products, arithmetic and copies ran while one was open for 0% of the time, Pallas kernels for 0%

profile of v1, /device:TPU:0, one launch (start us, length us, event | category | flops | bytes accessed | tf_op | source)
XLA Modules:
  0.0 427.6 jit_solution(7212926595785941592)
XLA Ops:
  6.5 2.0 fusion.2
  18.7 3.5 constant_dynamic-slice_fusion
  22.2 1.8 concatenate.18
  24.0 5.8 %fusion.3 = f32[1024,2048]{1,0:T(8,128)} fusion(f32[256,1024]{1,0:T(8,128)S(1)} %concatenate.18, f32[256,2048]{1,0:T(8,128)S(1)} %copy-done.3), kind=kOutput, calls=%fused_computation.34 | convolution fusion | flops 3221225472 | bytes 11534336 | tf_op jit(solution)/shard_map/dot_general | solution.py:126
  30.5 0.6 fusion
  31.1 0.6 broadcast_subtract_fusion
  32.0 105.2 %reduce-scatter.2.cloned.1.call-done = f32[64,2048]{1,0:T(8,128)} async-done(((f32[1024,2048]{1,0:T(8,128)}), f32[64,2048]{1,0:T(8,128)}) %reduce-scatter.2.cloned.1.call-update) | async-done | bytes 524304 | tf_op jit(solution)/shard_map/reduce_scatter | solution.py:133
  137.3 1.2 divide_bitcast_fusion
  138.6 1.9 collective-permute-done
  140.4 1.2 broadcast_select_fusion.7
  141.7 1.0 pad_maximum_fusion.3
  142.7 1.5 collective-permute-start.1
  144.2 24.0 %collective-permute-done.1 = f32[2,64,2048]{2,1,0:T(8,128)S(1)} collective-permute-done((f32[2,64,2048]{2,1,0:T(8,128)}, f32[2,64,2048]{2,1,0:T(8,128)S(1)}, u32[]{:S(2)}, u32[]{:S(2)}) %collective-permute-start.1) | collective-permute-done | bytes 1048608 | tf_op jit(solution)/shard_map/ppermute | solution.py:20
  168.4 0.9 copy-done.1
  169.5 0.2 copy-done.2
  169.7 1.7 collective-permute-start.2
  171.4 45.3 %collective-permute-done.2 = f32[4,64,2048]{2,1,0:T(8,128)} collective-permute-done((f32[4,64,2048]{2,1,0:T(8,128)S(1)}, f32[4,64,2048]{2,1,0:T(8,128)}, u32[]{:S(2)}, u32[]{:S(2)}) %collective-permute-start.2) | collective-permute-done | bytes 2097184 | tf_op jit(solution)/shard_map/ppermute | solution.py:20
  216.6 2.5 broadcast_select_fusion.3
  219.2 2.6 pad_maximum_fusion.1
  221.8 2.2 collective-permute-start.3
  224.0 179.8 %collective-permute-done.3 = f32[8,64,2048]{2,1,0:T(8,128)} collective-permute-done((f32[8,64,2048]{2,1,0:T(8,128)}, f32[8,64,2048]{2,1,0:T(8,128)}, u32[]{:S(2)}, u32[]{:S(2)}) %collective-permute-start.3) | collective-permute-done | bytes 4194336 | tf_op jit(solution)/shard_map/ppermute | solution.py:20
  403.8 7.6 %broadcast_select_fusion.1 = (f32[8,64,2048]{2,1,0:T(8,128)}, f32[8,64,2048]{2,1,0:T(8,128)}) fusion(f32[8,64,2048]{2,1,0:T(8,128)} %collective-permute-done.3, pred[]{:T(512)S(6)} %eq.23, f32[4,64,2048]{2,1,0:T(8,128)} %copy-done, f32[4,64,2048]{2,1,0:T(8,128)S(1)} %get-tuple-element.7), kind=kLoop, calls=%fused_computation.4 | loop fusion | flops 3145728 | bytes 16777216 | tf_op jit(solution)/shard_map/jit(_where)/select_n | solution.py:22
  411.4 4.0 pad_maximum_fusion
  415.5 5.2 %fusion.4 = f32[256,2048]{1,0:T(8,128)} fusion(f32[256,1024]{1,0:T(8,128)S(1)} %concatenate.18, f32[1024,2048]{1,0:T(8,128)S(1)} %bitcast.27), kind=kOutput, calls=%fused_computation.35 | convolution fusion | flops 3221225472 | bytes 11534336 | tf_op jit(solution)/shard_map/dot_general | solution.py:138
  (18 shorter events, 0.8 us)
Async XLA Ops:
  6.5 17.4 %copy-start.3 = (f32[256,2048]{1,0:T(8,128)S(1)}, f32[256,2048]{1,0:T(8,128)}, u32[]{:S(2)}) copy-start(f32[256,2048]{1,0:T(8,128)} %param.5) | copy-start | bytes 6291460
  6.5 130.7 %reduce-scatter.2.cloned.1.call-start = ((), (), s32[]{:S(2)}) async-start(), calls=%async_computation.1 | async-start | bytes 8912896 | tf_op jit(solution)/shard_map/reduce_scatter | solution.py:133
  29.8 0.7 copy-start.5
  29.8 1.3 copy-start.4
  138.5 2.0 collective-permute-start
  142.7 25.4 %collective-permute-start.1 = (f32[2,64,2048]{2,1,0:T(8,128)}, f32[2,64,2048]{2,1,0:T(8,128)S(1)}, u32[]{:S(2)}, u32[]{:S(2)}) collective-permute-start(f32[2,64,2048]{2,1,0:T(8,128)} %pad_maximum_fusion.3), channel_id=1, source_target_pairs={{0,2},{1,3},{2,0},{3,1},{4,6},{5,7},{6,4},{7,5},{8,10},{9,11},{10,... | collective-permute-start | bytes 3145736 | tf_op jit(solution)/shard_map/ppermute | solution.py:20
  168.3 1.0 copy-start.1
  168.3 1.3 copy-start.2
  169.7 46.9 %collective-permute-start.2 = (f32[4,64,2048]{2,1,0:T(8,128)S(1)}, f32[4,64,2048]{2,1,0:T(8,128)}, u32[]{:S(2)}, u32[]{:S(2)}) collective-permute-start(f32[4,64,2048]{2,1,0:T(8,128)S(1)} %pad_maximum_fusion.2), channel_id=1, source_target_pairs={{0,4},{1,5},{2,6},{3,7},{4,0},{5,1},{6,2},{7,3},{8,12},{9,13},{10,... | collective-permute-start | bytes 6291464 | tf_op jit(solution)/shard_map/ppermute | solution.py:20
  219.1 2.7 copy-start
  221.8 182.0 %collective-permute-start.3 = (f32[8,64,2048]{2,1,0:T(8,128)}, f32[8,64,2048]{2,1,0:T(8,128)}, u32[]{:S(2)}, u32[]{:S(2)}) collective-permute-start(f32[8,64,2048]{2,1,0:T(8,128)} %pad_maximum_fusion.1), channel_id=1, source_target_pairs={{0,8},{1,9},{2,10},{3,11},{4,12},{5,13},{6,14},{7,15},{8,0},{9,1},... | collective-permute-start | bytes 12582920 | tf_op jit(solution)/shard_map/ppermute | solution.py:20
Sparse Core Ops, SparseCore 0:
  29.9 107.2 reduce-scatter.1
